TPU v7x, 512 devices: a whole 4x4x16 slice. The times are simulated.
512 devices in a mesh: blk: 16 (over x_hi, y, core), dom: 32 (over z, x_lo).
Axes of the slice: x: 4 (x_hi: 2, x_lo: 2; x = x_hi * 2 + x_lo), y: 4, z: 16, core: 2. Of those that a mesh axis runs over, the one named last changes fastest.
Arguments:
- features: bfloat16 [32, 8192, 256], P('dom', 'blk'), may hold values from -6 to 6
- weight: bfloat16 [256, 256], replicated, may hold values from -0.375 to 0.375
- tiles: bfloat16 [32, 16, 16, 6, 128, 128], P('dom', 'blk'), may hold values from -0.15234375 to 0.15234375
- tile_pos: int32 [32, 16, 16, 6], P('dom', 'blk'), may hold values from 0 to 15, as said below
- tile_count: int32 [32, 16, 16], P('dom', 'blk'), may hold values from 1 to 6
- send_list: int32 [32, 16, 32, 32], P('dom', 'blk'), may hold values from 0 to 511
- send_count: int32 [32, 16, 32], P('dom', 'blk'), may hold values from 0 to 32, as said below
- owner_map: int32 [32, 16, 32, 32], P('dom', 'blk'), may hold values from 0 to 511
- halo_weight: float32 [32, 16, 32, 32], P('dom', 'blk'), may hold values from 0.25 to 1
- cotangent: bfloat16 [32, 8192, 256], P('dom', 'blk'), may hold values from -6 to 6
Outputs:
- layer_out: bfloat16 [32, 8192, 256], P('dom', 'blk')
- feature_grad: bfloat16 [32, 8192, 256], P('dom', 'blk')
- weight_grad: float32 [256, 256], replicated
Inputs may be any that keep to these rules, and one draw needn't show every extreme that they name: `tile_pos`: the 6 positions of one row group in one column group are distinct. `send_count`: zero where the peer is the sender's own partition.
All inputs are finite; a program needn't handle non-finite values.
Results may differ from a plain program's by a relative error of at most 0.019.
Values may be sent and summed in bfloat16 or wider, within the bound.
A program may use at most 128 MiB of HBM per device.

v0:
```python
import jax
import jax.numpy as jnp
from jax import lax
from jax.sharding import PartitionSpec as P


def spread_rows(tile_set, positions, counts, panel, per):
    groups, slots = positions.shape
    tile = tile_set.shape[-1]
    width = panel.shape[-1]
    grid = panel.reshape(groups, per, tile, width)
    column = positions % per
    row_tile = positions // per
    picked = grid[jnp.arange(groups)[:, None], column]
    product = jnp.einsum("gtij,gtjf->gtif", tile_set, picked, preferred_element_type=jnp.float32)
    live = jnp.arange(slots)[None, :] < counts[:, None]
    select = ((row_tile[..., None] == jnp.arange(per)[None, None, :]) & live[..., None]).astype(
        jnp.float32
    )
    return jnp.einsum("gtif,gtr->rif", product, select).reshape(per * tile, width)


def spread_cols(tile_set, positions, counts, grad_rows, per):
    groups, slots = positions.shape
    tile = tile_set.shape[-1]
    width = grad_rows.shape[-1]
    grid = grad_rows.reshape(per, tile, width)
    column = positions % per
    row_tile = positions // per
    picked = grid[row_tile]
    product = jnp.einsum("gtij,gtif->gtjf", tile_set, picked, preferred_element_type=jnp.float32)
    live = jnp.arange(slots)[None, :] < counts[:, None]
    select = ((column[..., None] == jnp.arange(per)[None, None, :]) & live[..., None]).astype(
        jnp.float32
    )
    return jnp.einsum("gtjf,gtc->gcjf", product, select).reshape(groups * per * tile, width)


def on_device(
    features,
    weight,
    tiles,
    tile_pos,
    tile_count,
    send_list,
    send_count,
    owner_map,
    halo_weight,
    cotangent,
):
    feats = features[0]
    rows, width = feats.shape
    tile_set = tiles[0, 0]
    positions = tile_pos[0, 0]
    counts = tile_count[0, 0]
    tile = tile_set.shape[-1]
    per = rows // tile
    send_rows = send_list[0, 0]
    send_live = send_count[0, 0]
    owners = owner_map[0, 0]
    edge_weight = halo_weight[0, 0]
    grad_in = cotangent[0]
    slots = send_rows.shape[1]
    live = (jnp.arange(slots)[None, :] < send_live[:, None])[..., None]
    empty = jnp.zeros((rows, width), jnp.float32)
    projected = jnp.dot(feats, weight, preferred_element_type=jnp.float32).astype(jnp.bfloat16)
    part_tiles = tile_set
    part_pos = positions
    part_count = counts
    local = spread_rows(
        part_tiles, part_pos, part_count, lax.all_gather(projected, "blk", axis=0, tiled=True), per
    )
    outgoing = jnp.where(live, projected[send_rows], jnp.zeros((), jnp.bfloat16))
    incoming = lax.all_to_all(outgoing, "dom", split_axis=0, concat_axis=0, tiled=True)
    weighted = edge_weight.reshape(-1, 1) * incoming.reshape(-1, width).astype(jnp.float32)
    halo_sum = empty.at[owners.reshape(-1)].add(weighted)
    layer_out = (local + halo_sum).astype(jnp.bfloat16)
    back = (edge_weight[..., None] * grad_in[owners].astype(jnp.float32)).astype(jnp.bfloat16)
    returned = lax.all_to_all(back, "dom", split_axis=0, concat_axis=0, tiled=True)
    returned = jnp.where(live, returned, jnp.zeros((), jnp.bfloat16))
    halo_back = empty.at[send_rows.reshape(-1)].add(returned.reshape(-1, width).astype(jnp.float32))
    part_tiles = tile_set
    part_pos = positions
    part_count = counts
    local_grad = lax.psum_scatter(
        spread_cols(part_tiles, part_pos, part_count, grad_in, per).astype(jnp.bfloat16),
        "blk",
        scatter_dimension=0,
        tiled=True,
    ).astype(jnp.float32)
    proj_grad = (local_grad + halo_back).astype(jnp.bfloat16)
    feature_grad = lax.dot_general(
        proj_grad, weight, (((1,), (1,)), ((), ())), preferred_element_type=jnp.float32
    )
    feature_grad = feature_grad.astype(jnp.bfloat16)
    weight_term = lax.dot_general(
        feats, proj_grad, (((0,), (0,)), ((), ())), preferred_element_type=jnp.float32
    )
    total = lax.psum(weight_term, ("blk", "dom"))
    scale = float(lax.axis_size("blk") * lax.axis_size("dom") * rows) ** (-0.5)
    return (layer_out[None], feature_grad[None], total * scale)


def solution(mesh):
    return jax.shard_map(
        on_device,
        mesh=mesh,
        in_specs=(
            P("dom", "blk", None),
            P(),
            P("dom", "blk", None, None, None, None),
            P("dom", "blk", None, None),
            P("dom", "blk", None),
            P("dom", "blk", None, None),
            P("dom", "blk", None),
            P("dom", "blk", None, None),
            P("dom", "blk", None, None),
            P("dom", "blk", None),
        ),
        out_specs=(P("dom", "blk", None), P("dom", "blk", None), P()),
        check_vma=False,
    )
```

profile of v0, /device:TPU:1, one launch (start us, length us, event | category | flops | bytes accessed | tf_op | source)
XLA Modules:
  0.0 745.6 jit_solution(18372749111417586942)
XLA Ops:
  7.2 1.4 compare_select_fusion.4
  8.7 1.3 add_select_fusion
  10.1 6.9 gather_fusion.2
  17.0 7.3 fusion.7
  24.3 11.7 %copy.29 = bf16[16,6,256,128]{2,1,3,0:T(8,128)(2,1)} copy(bf16[16,6,256,128]{3,2,1,0:T(8,128)(2,1)} %fusion.7) | data formatting | bytes 12582912 | tf_op jit(solution)/shard_map/gtij,gtif->gtjf/dot_general | solution.py:31
  36.2 5.7 fusion.4
  41.9 2.8 copy.25
  46.2 5.0 gather_fusion.3
  51.1 2.0 fusion.17
  53.2 17.1 %all-to-all-start.1 = ((bf16[32,32,256]{2,1,0:T(8,128)(2,1)}), bf16[32,32,256]{2,1,0:T(8,128)(2,1)}, u32[]{:S(2)}, u32[]{:S(2)}) async-start(bf16[32,32,256]{2,1,0:T(8,128)(2,1)} %fusion.17), calls=%async_computation.2 | async-start | bytes 1048576 | tf_op jit(solution)/shard_map/all_to_all | solution.py:79
  70.4 0.8 reshape_squeeze.12
  72.0 1.2 convolution_convert_fusion.1
  73.2 5.0 gather_fusion.1
  79.5 21.9 %all-to-all-done.1 = bf16[32,32,256]{2,1,0:T(8,128)(2,1)} async-done(((bf16[32,32,256]{2,1,0:T(8,128)(2,1)}), bf16[32,32,256]{2,1,0:T(8,128)(2,1)}, u32[]{:S(2)}, u32[]{:S(2)}) %all-to-all-start.1) | async-done | bytes 524320 | tf_op jit(solution)/shard_map/all_to_all | solution.py:79
  101.4 2.4 broadcast_select_fusion
  103.7 48.7 %reduce-scatter.2.cloned.1.call-done = bf16[512,256]{1,0:T(8,128)(2,1)} async-done(((bf16[8192,256]{1,0:T(8,128)(2,1)}), bf16[512,256]{1,0:T(8,128)(2,1)}) %reduce-scatter.2.cloned.1.call-update) | async-done | bytes 262160 | tf_op jit(solution)/shard_map/reduce_scatter | solution.py:85
  152.4 1.8 convert_element_type.47
  154.2 8.3 %scatter_custom_fusion.1 = f32[512,256]{1,0:T(8,128)} fusion(f32[512,256]{1,0:T(8,128)} %convert_element_type.47, s32[1024]{0:T(1024)} %bitcast.130, bf16[1024,256]{1,0:T(8,128)(2,1)} %bitcast.127), kind=kCustom, calls=%fused_computation.20 | custom fusion | flops 524288 | bytes 1048576 | tf_op jit(solution)/shard_map/scatter-add | solution.py:81
  162.5 2.1 convolution_bitcast_fusion
  166.9 12.4 %all-to-all-start = ((bf16[32,32,256]{2,1,0:T(8,128)(2,1)}), bf16[32,32,256]{2,1,0:T(8,128)(2,1)}, u32[]{:S(2)}, u32[]{:S(2)}) async-start(bf16[32,32,256]{2,1,0:T(8,128)(2,1)} %get-tuple-element.12), calls=%async_computation | async-start | bytes 1048576 | tf_op jit(solution)/shard_map/all_to_all | solution.py:74
  179.8 2.0 fusion.14
  181.8 444.9 %all-reduce.2.cloned.1.call-done = f32[256,256]{0,1:T(8,128)} async-done(((f32[256,256]{0,1:T(8,128)}), f32[256,256]{0,1:T(8,128)}) %all-reduce.2.cloned.1.call-update) | async-done | bytes 262160 | tf_op jit(solution)/shard_map/psum | solution.py:99
  626.7 1.0 broadcast_multiply_fusion
  627.7 0.8 copy.26
  628.5 70.2 %all-gather.2.cloned.1.call-done = bf16[8192,256]{1,0:T(8,128)(2,1)} async-done(((bf16[512,256]{1,0:T(8,128)(2,1)}), bf16[8192,256]{1,0:T(8,128)(2,1)}) %all-gather.2.cloned.1.call-update) | async-done | bytes 4194320 | tf_op jit(solution)/shard_map/all_gather | solution.py:71
  698.8 8.8 %gather_fusion = bf16[96,128,256]{2,1,0:T(8,128)(2,1)} fusion(bf16[16,4,128,256]{3,2,1,0:T(8,128)(2,1)} %bitcast.123, s32[96]{0:T(128)S(1)} %reshape.324), kind=kCustom, calls=%fused_computation | custom fusion | bytes 12583680 | tf_op jit(solution)/shard_map/gather | solution.py:14
  707.6 7.3 fusion.9
  714.8 9.1 %copy.27 = bf16[16,6,256,128]{2,0,1,3:T(8,128)(2,1)} copy(bf16[16,6,256,128]{3,2,1,0:T(8,128)(2,1)} %fusion.9) | data formatting | bytes 12582912 | tf_op jit(solution)/shard_map/gtij,gtjf->gtif/dot_general | solution.py:15
  723.9 3.8 fusion.11
  727.7 0.9 copy.22
  728.6 8.7 %scatter_custom_fusion = f32[512,256]{1,0:T(8,128)} fusion(f32[512,256]{1,0:T(8,128)} %bitcast.126, s32[1024]{0:T(1024)S(1)} %bitcast.129, bf16[1024,256]{1,0:T(8,128)(2,1)} %bitcast.31, f32[1024]{0:T(1024)S(1)} %mul.26), kind=kCustom, calls=%fused_computation.25 | custom fusion | flops 786432 | bytes 1052672 | tf_op jit(solution)/shard_map/scatter-add | solution.py:76
  737.3 1.8 convert_bitcast_fusion
  (49 shorter events, 6.7 us)
Async XLA Ops:
  7.2 9.8 %copy-start = (bf16[1,1,16,6,128,128]{5,4,3,2,1,0:T(8,128)(2,1)S(1)}, bf16[1,1,16,6,128,128]{5,4,3,2,1,0:T(8,128)(2,1)}, u32[]{:S(2)}) copy-start(bf16[1,1,16,6,128,128]{5,4,3,2,1,0:T(8,128)(2,1)} %param.12) | copy-start | bytes 9437188
  7.2 145.2 %reduce-scatter.2.cloned.1.call-start = ((), (), s32[]{:S(2)}) async-start(), calls=%async_computation.4 | async-start | bytes 4456448 | tf_op jit(solution)/shard_map/reduce_scatter | solution.py:85
  24.3 11.8 %copy-start.9 = (s32[1,1,16]{2,1,0:T(1,128)S(1)}, s32[1,1,16]{2,1,0:T(1,128)}, u32[]{:S(2)}) copy-start(s32[1,1,16]{2,1,0:T(1,128)} %param.14) | copy-start | bytes 196
  36.2 5.7 copy-start.5
  41.9 2.8 copy-start.4
  41.9 4.2 copy-start.1
  44.7 27.3 %copy-start.3 = (bf16[256,256]{1,0:T(8,128)(2,1)S(1)}, bf16[256,256]{1,0:T(8,128)(2,1)}, u32[]{:S(2)}) copy-start(bf16[256,256]{1,0:T(8,128)(2,1)} %param.11) | copy-start | bytes 393220
  53.2 48.2 %all-to-all-start.1 = ((bf16[32,32,256]{2,1,0:T(8,128)(2,1)}), bf16[32,32,256]{2,1,0:T(8,128)(2,1)}, u32[]{:S(2)}, u32[]{:S(2)}) async-start(bf16[32,32,256]{2,1,0:T(8,128)(2,1)} %fusion.17), calls=%async_computation.2 | async-start | bytes 1048576 | tf_op jit(solution)/shard_map/all_to_all | solution.py:79
  70.3 109.3 %copy-start.7 = (s32[16,6]{0,1:T(8,128)S(1)}, s32[16,6]{0,1:T(8,128)}, u32[]{:S(2)}) copy-start(s32[16,6]{0,1:T(8,128)} %get-tuple-element.14) | copy-start | bytes 1156
  70.3 109.4 %copy-start.6 = (pred[16,6]{1,0:T(8,128)(4,1)S(1)}, pred[16,6]{1,0:T(8,128)(4,1)}, u32[]{:S(2)}) copy-start(pred[16,6]{1,0:T(8,128)(4,1)} %copy-done.5) | copy-start | bytes 292
  70.3 556.4 %all-reduce.2.cloned.1.call-start = ((), (), s32[]{:S(2)}) async-start(), calls=%async_computation.5 | async-start | bytes 524288 | tf_op jit(solution)/shard_map/psum | solution.py:99
  73.2 91.5 %copy-start.2 = (bf16[512,256]{1,0:T(8,128)(2,1)}, bf16[512,256]{1,0:T(8,128)(2,1)S(1)}, u32[]{:S(2)}) copy-start(bf16[512,256]{1,0:T(8,128)(2,1)S(1)} %convolution_convert_fusion.1) | copy-start | bytes 786436
  79.5 99.9 %copy-start.8 = (s32[16,6,1]{0,2,1:T(1,128)S(1)}, s32[16,6,1]{0,2,1:T(1,128)}, u32[]{:S(2)}) copy-start(s32[16,6,1]{0,2,1:T(1,128)} %get-tuple-element.10) | copy-start | bytes 1156
  164.6 534.2 %all-gather.2.cloned.1.call-start = ((), (), s32[]{:S(2)}) async-start(), calls=%async_computation.3 | async-start | bytes 4456448 | tf_op jit(solution)/shard_map/all_gather | solution.py:71
  166.9 561.7 %all-to-all-start = ((bf16[32,32,256]{2,1,0:T(8,128)(2,1)}), bf16[32,32,256]{2,1,0:T(8,128)(2,1)}, u32[]{:S(2)}, u32[]{:S(2)}) async-start(bf16[32,32,256]{2,1,0:T(8,128)(2,1)} %get-tuple-element.12), calls=%async_computation | async-start | bytes 1048576 | tf_op jit(solution)/shard_map/all_to_all | solution.py:74
Sparse Core Ops, SparseCore 0:
  44.9 107.5 reduce-scatter.1
  164.7 461.9 all-reduce.1
  630.6 68.0 all-gather.1
where the time goes:
time: 747 us; the launch traced here: 746 us
  waiting for transfers between devices  586 us (78%)
  local copies, waits for them, and re-layouts  54.8 us (7%)
  other arithmetic  31.5 us (4%)
  starting transfers between devices  29.7 us (4%)
  matrix products  29.4 us (4%)
  between operations  13.9 us (2%)
    psum x1, waiting for transfers between devices, on_device(): total = lax.psum(weight_term, ('blk', 'dom'))  445 us
    all_gather x1, waiting for transfers between devices, on_device(): lax.all_gather(projected, 'blk', axis=0, tiled=True)  70.2 us
    reduce_scatter x1, waiting for transfers between devices, on_device(): lax.psum_scatter(spread_cols(part_tiles, part_pos, part_count, grad_in, p...  48.7 us
    all_to_all x1, waiting for transfers between devices, on_device(): lax.all_to_all(back, 'dom', split_axis=0, concat_axis=0, tiled=True)  21.9 us
    all_to_all x1, starting transfers between devices, on_device(): lax.all_to_all(back, 'dom', split_axis=0, concat_axis=0, tiled=True)  17.1 us
  transfers between devices with their start and end apart: 5, of which 4 were waited for; matrix products, arithmetic and copies ran while one was open for 7% of the time, Pallas kernels for 0%

commit v1 on v0

--- a/solution.py
+++ b/solution.py
@@ -96,7 +96,7 @@
     weight_term = lax.dot_general(
         feats, proj_grad, (((0,), (0,)), ((), ())), preferred_element_type=jnp.float32
     )
-    total = lax.psum(weight_term, ("blk", "dom"))
+    total = lax.psum(lax.psum(weight_term, "blk"), "dom")
     scale = float(lax.axis_size("blk") * lax.axis_size("dom") * rows) ** (-0.5)
     return (layer_out[None], feature_grad[None], total * scale)
 

time: 747 us -> 708 us (0.948)
  waiting for transfers between devices: 586 us -> 547 us
    psum x1 -> x2, waiting for transfers between devices: 445 us -> 383 us  [on_device(): total = lax.psum(lax.psum(weight_term, 'blk'), 'dom')]
    all_gather x1, waiting for transfers between devices: 70.2 us -> 92.6 us  [on_device(): lax.all_gather(projected, 'blk', axis=0, tiled=True)]
  transfers between devices with their start and end apart: 5 -> 6, of which waited for: 4 -> 5; matrix products, arithmetic and copies ran while one was open for 7% -> 8% of each run, Pallas kernels for 0% -> 0%
where the time goes in v1:
time: 708 us; the launch traced here: 707 us
  waiting for transfers between devices  547 us (77%)
  local copies, waits for them, and re-layouts  54.8 us (8%)
  other arithmetic  31.5 us (4%)
  starting transfers between devices  29.7 us (4%)
  matrix products  29.4 us (4%)
  between operations  13.9 us (2%)
    psum x2, waiting for transfers between devices, on_device(): total = lax.psum(lax.psum(weight_term, 'blk'), 'dom')  383 us
    all_gather x1, waiting for transfers between devices, on_device(): lax.all_gather(projected, 'blk', axis=0, tiled=True)  92.6 us
    reduce_scatter x1, waiting for transfers between devices, on_device(): lax.psum_scatter(spread_cols(part_tiles, part_pos, part_count, grad_in, p...  48.7 us
    all_to_all x1, waiting for transfers between devices, on_device(): lax.all_to_all(back, 'dom', split_axis=0, concat_axis=0, tiled=True)  21.9 us
    all_to_all x1, starting transfers between devices, on_device(): lax.all_to_all(back, 'dom', split_axis=0, concat_axis=0, tiled=True)  17.1 us
  transfers between devices with their start and end apart: 6, of which 5 were waited for; matrix products, arithmetic and copies ran while one was open for 8% of the time, Pallas kernels for 0%

profile of v1, /device:TPU:1, one launch (start us, length us, event | category | flops | bytes accessed | tf_op | source)
XLA Modules:
  0.0 706.5 jit_solution(11339113620269608713)
XLA Ops:
  7.2 1.4 compare_select_fusion.4
  8.7 1.3 add_select_fusion
  10.1 6.9 gather_fusion.2
  17.0 7.3 %fusion.7 = bf16[16,6,256,128]{3,2,1,0:T(8,128)(2,1)} fusion(bf16[16,6,128,256]{3,2,1,0:T(8,128)(2,1)} %bitcast.121, bf16[1,1,16,6,128,128]{5,4,3,2,1,0:T(8,128)(2,1)S(1)} %copy-done), kind=kOutput, calls=%fused_computation.11 | convolution fusion | flops 805306368 | bytes 15728640 | tf_op jit(solution)/shard_map/gtij,gtif->gtjf/dot_general | solution.py:31
  24.3 11.7 %copy.29 = bf16[16,6,256,128]{2,1,3,0:T(8,128)(2,1)} copy(bf16[16,6,256,128]{3,2,1,0:T(8,128)(2,1)} %fusion.7) | data formatting | bytes 12582912 | tf_op jit(solution)/shard_map/gtij,gtif->gtjf/dot_general | solution.py:31
  36.2 5.7 fusion.4
  41.9 2.8 copy.25
  46.2 5.0 gather_fusion.3
  51.1 2.0 fusion.17
  53.2 17.1 %all-to-all-start.1 = ((bf16[32,32,256]{2,1,0:T(8,128)(2,1)}), bf16[32,32,256]{2,1,0:T(8,128)(2,1)}, u32[]{:S(2)}, u32[]{:S(2)}) async-start(bf16[32,32,256]{2,1,0:T(8,128)(2,1)} %fusion.17), calls=%async_computation.2 | async-start | bytes 1048576 | tf_op jit(solution)/shard_map/all_to_all | solution.py:79
  72.0 1.2 convolution_convert_fusion.1
  73.2 5.0 gather_fusion.1
  79.5 21.9 %all-to-all-done.1 = bf16[32,32,256]{2,1,0:T(8,128)(2,1)} async-done(((bf16[32,32,256]{2,1,0:T(8,128)(2,1)}), bf16[32,32,256]{2,1,0:T(8,128)(2,1)}, u32[]{:S(2)}, u32[]{:S(2)}) %all-to-all-start.1) | async-done | bytes 524320 | tf_op jit(solution)/shard_map/all_to_all | solution.py:79
  101.4 2.4 broadcast_select_fusion
  103.7 48.7 %reduce-scatter.2.cloned.1.call-done = bf16[512,256]{1,0:T(8,128)(2,1)} async-done(((bf16[8192,256]{1,0:T(8,128)(2,1)}), bf16[512,256]{1,0:T(8,128)(2,1)}) %reduce-scatter.2.cloned.1.call-update) | async-done | bytes 262160 | tf_op jit(solution)/shard_map/reduce_scatter | solution.py:85
  152.4 1.8 convert_element_type.47
  154.2 8.3 %scatter_custom_fusion.1 = f32[512,256]{1,0:T(8,128)} fusion(f32[512,256]{1,0:T(8,128)} %convert_element_type.47, s32[1024]{0:T(1024)} %bitcast.130, bf16[1024,256]{1,0:T(8,128)(2,1)} %bitcast.127), kind=kCustom, calls=%fused_computation.20 | custom fusion | flops 524288 | bytes 1048576 | tf_op jit(solution)/shard_map/scatter-add | solution.py:81
  162.5 2.1 convolution_bitcast_fusion
  164.6 153.4 %all-reduce.3.cloned.1.call-done = f32[256,256]{0,1:T(8,128)} async-done(((f32[256,256]{0,1:T(8,128)}), f32[256,256]{0,1:T(8,128)}) %all-reduce.3.cloned.1.call-update) | async-done | bytes 262160 | tf_op jit(solution)/shard_map/psum | solution.py:99
  320.3 12.4 %all-to-all-start = ((bf16[32,32,256]{2,1,0:T(8,128)(2,1)}), bf16[32,32,256]{2,1,0:T(8,128)(2,1)}, u32[]{:S(2)}, u32[]{:S(2)}) async-start(bf16[32,32,256]{2,1,0:T(8,128)(2,1)} %get-tuple-element.12), calls=%async_computation | async-start | bytes 1048576 | tf_op jit(solution)/shard_map/all_to_all | solution.py:74
  333.1 2.0 fusion.14
  335.2 230.1 %all-reduce.5.cloned.1.call-done = f32[256,256]{0,1:T(8,128)} async-done(((f32[256,256]{0,1:T(8,128)}), f32[256,256]{0,1:T(8,128)}) %all-reduce.5.cloned.1.call-update) | async-done | bytes 262160 | tf_op jit(solution)/shard_map/psum | solution.py:99
  565.2 1.0 broadcast_multiply_fusion
  566.2 0.8 copy.26
  567.0 92.6 %all-gather.2.cloned.1.call-done = bf16[8192,256]{1,0:T(8,128)(2,1)} async-done(((bf16[512,256]{1,0:T(8,128)(2,1)}), bf16[8192,256]{1,0:T(8,128)(2,1)}) %all-gather.2.cloned.1.call-update) | async-done | bytes 4194320 | tf_op jit(solution)/shard_map/all_gather | solution.py:71
  659.6 8.8 %gather_fusion = bf16[96,128,256]{2,1,0:T(8,128)(2,1)} fusion(bf16[16,4,128,256]{3,2,1,0:T(8,128)(2,1)} %bitcast.123, s32[96]{0:T(128)S(1)} %reshape.324), kind=kCustom, calls=%fused_computation | custom fusion | bytes 12583680 | tf_op jit(solution)/shard_map/gather | solution.py:14
  668.4 7.3 %fusion.9 = bf16[16,6,256,128]{3,2,1,0:T(8,128)(2,1)} fusion(bf16[16,6,128,256]{3,2,1,0:T(8,128)(2,1)} %bitcast.120, bf16[1,1,16,6,128,128]{5,4,3,2,1,0:T(8,128)(2,1)S(1)} %copy-done), kind=kOutput, calls=%fused_computation.13 | convolution fusion | flops 805306368 | bytes 15728640 | tf_op jit(solution)/shard_map/gtij,gtjf->gtif/dot_general | solution.py:15
  675.7 9.1 %copy.27 = bf16[16,6,256,128]{2,0,1,3:T(8,128)(2,1)} copy(bf16[16,6,256,128]{3,2,1,0:T(8,128)(2,1)} %fusion.9) | data formatting | bytes 12582912 | tf_op jit(solution)/shard_map/gtij,gtjf->gtif/dot_general | solution.py:15
  684.8 3.8 fusion.11
  688.6 0.9 copy.22
  689.5 8.7 %scatter_custom_fusion = f32[512,256]{1,0:T(8,128)} fusion(f32[512,256]{1,0:T(8,128)} %bitcast.126, s32[1024]{0:T(1024)S(1)} %bitcast.129, bf16[1024,256]{1,0:T(8,128)(2,1)} %bitcast.31, f32[1024]{0:T(1024)S(1)} %mul.26), kind=kCustom, calls=%fused_computation.25 | custom fusion | flops 786432 | bytes 1052672 | tf_op jit(solution)/shard_map/scatter-add | solution.py:76
  698.2 1.8 convert_bitcast_fusion
  (52 shorter events, 7.4 us)
Async XLA Ops:
  7.2 9.8 %copy-start = (bf16[1,1,16,6,128,128]{5,4,3,2,1,0:T(8,128)(2,1)S(1)}, bf16[1,1,16,6,128,128]{5,4,3,2,1,0:T(8,128)(2,1)}, u32[]{:S(2)}) copy-start(bf16[1,1,16,6,128,128]{5,4,3,2,1,0:T(8,128)(2,1)} %param.12) | copy-start | bytes 9437188
  7.2 145.2 %reduce-scatter.2.cloned.1.call-start = ((), (), s32[]{:S(2)}) async-start(), calls=%async_computation.4 | async-start | bytes 4456448 | tf_op jit(solution)/shard_map/reduce_scatter | solution.py:85
  24.3 11.8 %copy-start.9 = (s32[1,1,16]{2,1,0:T(1,128)S(1)}, s32[1,1,16]{2,1,0:T(1,128)}, u32[]{:S(2)}) copy-start(s32[1,1,16]{2,1,0:T(1,128)} %param.14) | copy-start | bytes 196
  36.2 5.7 copy-start.5
  41.9 2.8 copy-start.4
  41.9 4.2 copy-start.1
  44.7 27.3 %copy-start.3 = (bf16[256,256]{1,0:T(8,128)(2,1)S(1)}, bf16[256,256]{1,0:T(8,128)(2,1)}, u32[]{:S(2)}) copy-start(bf16[256,256]{1,0:T(8,128)(2,1)} %param.11) | copy-start | bytes 393220
  53.2 48.2 %all-to-all-start.1 = ((bf16[32,32,256]{2,1,0:T(8,128)(2,1)}), bf16[32,32,256]{2,1,0:T(8,128)(2,1)}, u32[]{:S(2)}, u32[]{:S(2)}) async-start(bf16[32,32,256]{2,1,0:T(8,128)(2,1)} %fusion.17), calls=%async_computation.2 | async-start | bytes 1048576 | tf_op jit(solution)/shard_map/all_to_all | solution.py:79
  70.3 262.6 %copy-start.7 = (s32[16,6]{0,1:T(8,128)S(1)}, s32[16,6]{0,1:T(8,128)}, u32[]{:S(2)}) copy-start(s32[16,6]{0,1:T(8,128)} %get-tuple-element.14) | copy-start | bytes 1156
  70.3 262.7 %copy-start.6 = (pred[16,6]{1,0:T(8,128)(4,1)S(1)}, pred[16,6]{1,0:T(8,128)(4,1)}, u32[]{:S(2)}) copy-start(pred[16,6]{1,0:T(8,128)(4,1)} %copy-done.5) | copy-start | bytes 292
  70.3 247.7 %all-reduce.3.cloned.1.call-start = ((), (), s32[]{:S(2)}) async-start(), calls=%async_computation.5 | async-start | bytes 524288 | tf_op jit(solution)/shard_map/psum | solution.py:99
  73.2 245.0 %copy-start.2 = (bf16[512,256]{1,0:T(8,128)(2,1)}, bf16[512,256]{1,0:T(8,128)(2,1)S(1)}, u32[]{:S(2)}) copy-start(bf16[512,256]{1,0:T(8,128)(2,1)S(1)} %convolution_convert_fusion.1) | copy-start | bytes 786436
  79.5 253.2 %copy-start.8 = (s32[16,6,1]{0,2,1:T(1,128)S(1)}, s32[16,6,1]{0,2,1:T(1,128)}, u32[]{:S(2)}) copy-start(s32[16,6,1]{0,2,1:T(1,128)} %get-tuple-element.10) | copy-start | bytes 1156
  164.6 400.6 %all-reduce.5.cloned.1.call-start = ((), (), s32[]{:S(2)}) async-start(), calls=%async_computation.6 | async-start | bytes 524288 | tf_op jit(solution)/shard_map/psum | solution.py:99
  318.1 341.5 %all-gather.2.cloned.1.call-start = ((), (), s32[]{:S(2)}) async-start(), calls=%async_computation.3 | async-start | bytes 4456448 | tf_op jit(solution)/shard_map/all_gather | solution.py:71
  320.3 369.2 %all-to-all-start = ((bf16[32,32,256]{2,1,0:T(8,128)(2,1)}), bf16[32,32,256]{2,1,0:T(8,128)(2,1)}, u32[]{:S(2)}, u32[]{:S(2)}) async-start(bf16[32,32,256]{2,1,0:T(8,128)(2,1)} %get-tuple-element.12), calls=%async_computation | async-start | bytes 1048576 | tf_op jit(solution)/shard_map/all_to_all | solution.py:74
Sparse Core Ops, SparseCore 0:
  44.9 107.5 reduce-scatter.1
  164.7 153.3 all-reduce.2
  321.0 244.2 all-reduce.4
  569.5 90.0 all-gather.1
